TPU v7x, 512 devices: a whole 4x4x16 slice. The times are simulated.
512 devices in a mesh: dp: 16 (over y, x), expert: 32 (over z, core).
Axes of the slice: x: 4, y: 4, z: 16, core: 2. Of those that a mesh axis runs over, the one named last changes fastest.
Arguments:
- tokens: bfloat16 [32768, 2048], P(('dp', 'expert')), may hold values from -6 to 6
- route_ids: int32 [32768, 8], P(('dp', 'expert')), may hold values from 0 to 127, all different within a row; in each aligned block of 64 rows (0 to 63, 64 to 127, ...) at most 8 rows name the same one
- route_weights: bfloat16 [32768, 8], P(('dp', 'expert')), may hold values from 0.099609375 to 0.5
- placement: int32 [128], replicated, may hold values from 0 to 127, each once
- gate_proj: bfloat16 [16, 32, 1, 192, 2048], P('dp', 'expert'), may hold values from -0.125 to 0.125
- up_proj: bfloat16 [16, 32, 1, 192, 2048], P('dp', 'expert'), may hold values from -0.125 to 0.125
- down_proj: bfloat16 [16, 32, 1, 192, 2048], P('dp', 'expert'), may hold values from -0.21875 to 0.21875
Outputs:
- mixed: bfloat16 [32768, 2048], P(('dp', 'expert'))
Inputs may be any that keep to these rules, and one draw needn't show every extreme that they name: `route_ids`: the 8 ids of a token differ. Among the rows of one device no expert is named more than 8 times, and in every draw some expert is named exactly 8 times by the rows of some device. `placement`: each slot holds exactly one expert.
All inputs are finite; a program needn't handle non-finite values.
Results may differ from a plain program's by a relative error of at most 0.0058.
Values may be sent and summed in bfloat16 or wider, within the bound.
A program may use at most 128 MiB of HBM per device.

v0:
```python
import jax
import jax.numpy as jnp
from jax import lax
from jax.sharding import PartitionSpec as P

CAP = 8


def swapped(value, axis, stride):
    mask = 2**stride
    pairs = [(source, source ^ mask) for source in range(lax.axis_size(axis))]
    return lax.ppermute(value, axis, pairs)


def project(rows, gate_w, up_w, down_w):
    gate = jnp.einsum("bkcd,kfd->bkcf", rows, gate_w, preferred_element_type=jnp.float32)
    up = jnp.einsum("bkcd,kfd->bkcf", rows, up_w, preferred_element_type=jnp.float32)
    hidden = (jax.nn.silu(gate) * up).astype(jnp.bfloat16)
    return jnp.einsum("bkcf,kfd->bkcd", hidden, down_w, preferred_element_type=jnp.float32)


def on_device(tokens, route_ids, route_weights, placement, gate_proj, up_proj, down_proj):
    n_rows = lax.axis_size("dp")
    n_cols = lax.axis_size("expert")
    groups = n_cols // 4
    subsets = n_rows // 4
    per_slot = gate_proj.shape[2]
    width = tokens.shape[1]
    tok_count = tokens.shape[0]
    topk = route_ids.shape[1]
    experts = placement.shape[0]
    capacity = CAP
    expert_hot = (
        route_ids[:, :, None] == jnp.arange(experts, dtype=jnp.int32)[None, None, :]
    ).astype(jnp.int32)
    slot_ids = jnp.sum(expert_hot * placement[None, None, :], axis=2)
    flat_hot = expert_hot.reshape(tok_count * topk, experts)
    earlier = jnp.cumsum(flat_hot, axis=0) - flat_hot
    position = jnp.sum(earlier * flat_hot, axis=1).reshape(tok_count, topk)
    row_of = slot_ids // (groups * per_slot)
    group_of = slot_ids // per_slot % groups
    inner_of = slot_ids % per_slot
    target = (group_of * (n_rows * per_slot) + row_of * per_slot + inner_of) * capacity + position
    buffer_rows = experts * capacity
    lanes = jnp.arange(buffer_rows, dtype=jnp.int32)
    matches = target[None, :, :] == lanes[:, None, None]
    dispatch = jnp.sum(matches.astype(jnp.int32), axis=2).astype(jnp.bfloat16)
    outgoing = jnp.dot(dispatch, tokens, preferred_element_type=jnp.float32).astype(jnp.bfloat16)
    outgoing = outgoing.reshape(groups, n_rows * per_slot, capacity, width)
    by_rows = lax.all_to_all(outgoing, "dp", split_axis=1, concat_axis=1, tiled=True)
    by_rows = by_rows.reshape(n_cols, subsets * per_slot, capacity, width)
    arrived = lax.all_to_all(by_rows, "expert", split_axis=0, concat_axis=0, tiled=True)
    arrived = arrived.reshape(n_cols * subsets, per_slot, capacity, width)
    own_gate = gate_proj[0, 0]
    own_up = up_proj[0, 0]
    own_down = down_proj[0, 0]
    far_gate, far_up, far_down = swapped((own_gate, own_up, own_down), "expert", 1)
    gate_half = jnp.concatenate([own_gate, far_gate], axis=1)
    up_half = jnp.concatenate([own_up, far_up], axis=1)
    down_half = jnp.concatenate([own_down, far_down], axis=1)
    partner_rows = swapped(arrived, "expert", 0)
    partner_part = project(partner_rows, gate_half, up_half, down_half)
    returned = swapped(partner_part, "expert", 0)
    own_part = project(arrived, gate_half, up_half, down_half)
    result = (own_part + returned).astype(jnp.bfloat16)
    result = result.reshape(n_cols, subsets * per_slot, capacity, width)
    going_back = lax.all_to_all(result, "expert", split_axis=0, concat_axis=0, tiled=True)
    going_back = going_back.reshape(groups, n_rows * per_slot, capacity, width)
    at_home = lax.all_to_all(going_back, "dp", split_axis=1, concat_axis=1, tiled=True)
    flat_rows = at_home.reshape(buffer_rows, width)
    picked = target[:, :, None] == lanes[None, None, :]
    mixing = jnp.sum(
        jnp.where(picked, route_weights[:, :, None], jnp.zeros((), jnp.bfloat16)), axis=1
    )
    return jnp.dot(mixing, flat_rows, preferred_element_type=jnp.float32).astype(jnp.bfloat16)


def solution(mesh):
    in_specs = (
        P(("dp", "expert"), None),
        P(("dp", "expert"), None),
        P(("dp", "expert"), None),
        P(),
        P("dp", "expert", None, None, None),
        P("dp", "expert", None, None, None),
        P("dp", "expert", None, None, None),
    )
    out_specs = P(("dp", "expert"), None)
    return jax.shard_map(
        on_device, mesh=mesh, in_specs=in_specs, out_specs=out_specs, check_vma=False
    )
```

profile of v0, /device:TPU:1, one launch (start us, length us, event | category | flops | bytes accessed | tf_op | source)
XLA Modules:
  0.0 671.7 jit_solution(16818391591064527323)
XLA Ops:
  6.3 57.9 %all_to_all.20 = bf16[8,16,8,2048]{3,2,0,1:T(8,128)(2,1)S(1)} all-to-all(bf16[8,16,8,2048]{3,2,0,1:T(8,128)(2,1)S(1)} %copy.67), channel_id=1, replica_groups=mesh['dp'=16,'expert'=32] {'dp'}, dimensions={1} | all-to-all | bytes 8388608 | tf_op jit(solution)/shard_map/all_to_all | solution.py:50
  64.5 4.0 copy.69
  68.5 206.9 %all_to_all.21 = bf16[32,4,8,2048]{3,1,2,0:T(4,128)(2,1)S(1)} all-to-all(bf16[32,4,8,2048]{3,1,2,0:T(4,128)(2,1)S(1)} %copy.69), channel_id=1, replica_groups=mesh['dp'=16,'expert'=32] {'expert'}, dimensions={0} | all-to-all | bytes 8388608 | tf_op jit(solution)/shard_map/all_to_all | solution.py:52
  275.4 4.0 copy.70
  279.4 7.1 %reshape.159 = bf16[128,1,8,2048]{3,0,2,1:T(8,128)(2,1)} reshape(bf16[32,4,8,2048]{3,1,0,2:T(4,128)(2,1)} %copy.70) | data formatting | bytes 8388608 | tf_op jit(solution)/shard_map/reshape | solution.py:53
  286.4 2.4 collective-permute-start.3
  290.8 3.4 collective-permute-start.2
  296.3 13.6 %collective-permute-done.1 = bf16[1,192,2048]{2,1,0:T(8,128)(2,1)S(1)} collective-permute-done((bf16[1,192,2048]{2,1,0:T(8,128)(2,1)S(1)}, bf16[1,192,2048]{2,1,0:T(8,128)(2,1)S(1)}, u32[]{:S(2)}, u32[]{:S(2)}) %collective-permute-start.1) | collective-permute-done | bytes 786464 | tf_op jit(solution)/shard_map/ppermute | solution.py:12
  309.9 3.0 fusion.3
  312.9 13.8 %collective-permute-done.2 = bf16[1,192,2048]{2,1,0:T(8,128)(2,1)S(1)} collective-permute-done((bf16[1,192,2048]{2,1,0:T(8,128)(2,1)S(1)}, bf16[1,192,2048]{2,1,0:T(8,128)(2,1)S(1)}, u32[]{:S(2)}, u32[]{:S(2)}) %collective-permute-start.2) | collective-permute-done | bytes 786464 | tf_op jit(solution)/shard_map/ppermute | solution.py:12
  327.6 16.1 %collective-permute-done = bf16[1,192,2048]{2,1,0:T(8,128)(2,1)} collective-permute-done((bf16[1,192,2048]{2,1,0:T(8,128)(2,1)S(1)}, bf16[1,192,2048]{2,1,0:T(8,128)(2,1)}, u32[]{:S(2)}, u32[]{:S(2)}) %collective-permute-start) | collective-permute-done | bytes 786464 | tf_op jit(solution)/shard_map/ppermute | solution.py:12
  343.7 10.4 %convolution_bitcast_fusion = f32[128,1,8,2048]{3,0,2,1:T(8,128)} fusion(bf16[128,1,8,2048]{3,0,2,1:T(8,128)(2,1)} %copy-done.3, f32[384,128,8]{1,0,2:T(8,128)} %fusion.3, bf16[1,192,2048]{2,1,0:T(8,128)(2,1)} %copy-done.8, bf16[1,192,2048]{2,1,0:T(8,128)(2,1)S(1)} %bitcast.151, bf16[1,192,2048]{2,1,0:T(8,128)(2,1)} %collective-permute-done, ...), kind=kOutput, calls=%fused_computation.2 | convolution fusion | flops 3229876224 | bytes 17301504 | tf_op jit(solution)/shard_map/bkcf,kfd->bkcd/dot_general | solution.py:19
  354.1 2.7 collective-permute-start.4
  356.8 6.9 %reshape.156 = bf16[128,8,2048]{2,0,1:T(8,128)(2,1)} reshape(bf16[32,4,8,2048]{3,1,0,2:T(4,128)(2,1)} %copy.70) | data formatting | bytes 8388608 | tf_op jit(solution)/shard_map/reshape.4
  363.8 5.4 fusion.24
  369.2 10.4 %fusion.20 = f32[2048,128,8]{0,1,2:T(8,128)} fusion(bf16[128,8,2048]{2,0,1:T(8,128)(2,1)} %reshape.156, f32[384,128,8]{1,0,2:T(8,128)} %fusion.24, bf16[1,192,2048]{2,1,0:T(8,128)(2,1)} %copy-done.8, bf16[1,192,2048]{2,1,0:T(8,128)(2,1)S(1)} %bitcast.152, bf16[1,192,2048]{2,1,0:T(8,128)(2,1)} %collective-permute-done, bf16[1,192,2048]{2,1,0:T(8,128)(2,1)S(1)} %bitcast.155), kind=kOutput, calls=%fused_computation.32 | convolution fusion | flops 3229876224 | bytes 17301504 | tf_op jit(solution)/shard_map/bkcf,kfd->bkcd/dot_general | solution.py:19
  379.6 9.1 %fusion = bf16[128,1,8,2048]{3,0,2,1:T(8,128)(2,1)} fusion(f32[128,1,8,2048]{3,0,2,1:T(8,128)} %collective-permute-done.4, f32[2048,128,8]{0,1,2:T(8,128)} %fusion.20), kind=kLoop, calls=%fused_computation.1 | loop fusion | flops 4194304 | bytes 20971520 | tf_op jit(solution)/shard_map/convert_element_type | solution.py:65
  388.8 7.2 %reshape.162 = bf16[32,4,8,2048]{3,1,0,2:T(4,128)(2,1)} reshape(bf16[128,1,8,2048]{3,0,2,1:T(8,128)(2,1)} %fusion) | data formatting | bytes 8388608 | tf_op jit(solution)/shard_map/reshape | solution.py:66
  396.0 4.3 copy.76
  400.2 193.6 %all_to_all.22 = bf16[32,4,8,2048]{3,1,2,0:T(4,128)(2,1)S(1)} all-to-all(bf16[32,4,8,2048]{3,1,2,0:T(4,128)(2,1)S(1)} %copy.76), channel_id=1, replica_groups=mesh['dp'=16,'expert'=32] {'expert'}, dimensions={0} | all-to-all | bytes 8388608 | tf_op jit(solution)/shard_map/all_to_all | solution.py:67
  593.8 4.4 copy.77
  600.5 4.7 all-to-all-start.3
  606.0 61.6 %all-to-all-done.3 = bf16[8,16,8,2048]{3,2,0,1:T(8,128)(2,1)} async-done(((bf16[8,16,8,2048]{3,2,0,1:T(8,128)(2,1)}), bf16[8,16,8,2048]{3,2,0,1:T(8,128)(2,1)}, u32[]{:S(2)}, u32[]{:S(2)}) %all-to-all-start.3) | async-done | bytes 4194336 | tf_op jit(solution)/shard_map/all_to_all | solution.py:69
  667.6 2.5 copy.79
  (45 shorter events, 16.1 us)
Async XLA Ops:
  0.0 4.4 copy-start
  279.4 9.5 %copy-start.4 = (bf16[1,1,1,192,2048]{4,3,2,1,0:T(8,128)(2,1)S(1)}, bf16[1,1,1,192,2048]{4,3,2,1,0:T(8,128)(2,1)}, u32[]{:S(2)}) copy-start(bf16[1,1,1,192,2048]{4,3,2,1,0:T(8,128)(2,1)} %param.11) | copy-start | bytes 2359300
  279.4 11.4 %copy-start.5 = (bf16[1,1,1,192,2048]{4,3,2,1,0:T(8,128)(2,1)S(1)}, bf16[1,1,1,192,2048]{4,3,2,1,0:T(8,128)(2,1)}, u32[]{:S(2)}) copy-start(bf16[1,1,1,192,2048]{4,3,2,1,0:T(8,128)(2,1)} %param.12) | copy-start | bytes 2359300
  279.4 14.8 %copy-start.6 = (bf16[1,1,1,192,2048]{4,3,2,1,0:T(8,128)(2,1)S(1)}, bf16[1,1,1,192,2048]{4,3,2,1,0:T(8,128)(2,1)}, u32[]{:S(2)}) copy-start(bf16[1,1,1,192,2048]{4,3,2,1,0:T(8,128)(2,1)} %param.13) | copy-start | bytes 2359300
  286.4 23.5 %collective-permute-start.3 = (bf16[128,1,8,2048]{3,0,2,1:T(8,128)(2,1)}, bf16[128,1,8,2048]{3,0,2,1:T(8,128)(2,1)S(1)}, u32[]{:S(2)}, u32[]{:S(2)}) collective-permute-start(bf16[128,1,8,2048]{3,0,2,1:T(8,128)(2,1)} %reshape.159), channel_id=1, source_target_pairs={{0,1},{1,0},{2,3},{3,2},{4,5},{5,4},{6,7},{7,6},{8,9},{9,8},{10,11... | collective-permute-start | bytes 12582920 | tf_op jit(solution)/shard_map/ppermute | solution.py:12
  288.8 21.1 %collective-permute-start.1 = (bf16[1,192,2048]{2,1,0:T(8,128)(2,1)S(1)}, bf16[1,192,2048]{2,1,0:T(8,128)(2,1)S(1)}, u32[]{:S(2)}, u32[]{:S(2)}) collective-permute-start(bf16[1,192,2048]{2,1,0:T(8,128)(2,1)S(1)} %bitcast.147), channel_id=1, source_target_pairs={{0,2},{1,3},{2,0},{3,1},{4,6},{5,7},{6,4},{7,5},{8,10},{9,11},{10,... | collective-permute-start | bytes 2359304 | tf_op jit(solution)/shard_map/ppermute | solution.py:12
  290.8 36.0 %collective-permute-start.2 = (bf16[1,192,2048]{2,1,0:T(8,128)(2,1)S(1)}, bf16[1,192,2048]{2,1,0:T(8,128)(2,1)S(1)}, u32[]{:S(2)}, u32[]{:S(2)}) collective-permute-start(bf16[1,192,2048]{2,1,0:T(8,128)(2,1)S(1)} %bitcast.150), channel_id=1, source_target_pairs={{0,2},{1,3},{2,0},{3,1},{4,6},{5,7},{6,4},{7,5},{8,10},{9,11},{10,... | collective-permute-start | bytes 2359304 | tf_op jit(solution)/shard_map/ppermute | solution.py:12
  294.2 49.5 %collective-permute-start = (bf16[1,192,2048]{2,1,0:T(8,128)(2,1)S(1)}, bf16[1,192,2048]{2,1,0:T(8,128)(2,1)}, u32[]{:S(2)}, u32[]{:S(2)}) collective-permute-start(bf16[1,192,2048]{2,1,0:T(8,128)(2,1)S(1)} %bitcast.153), channel_id=1, source_target_pairs={{0,2},{1,3},{2,0},{3,1},{4,6},{5,7},{6,4},{7,5},{8,10},{9,11},{10,... | collective-permute-start | bytes 2359304 | tf_op jit(solution)/shard_map/ppermute | solution.py:12
  309.9 3.0 copy-start.7
  309.9 3.0 copy-start.3
  326.7 0.9 copy-start.8
  354.1 25.5 %collective-permute-start.4 = (f32[128,1,8,2048]{3,0,2,1:T(8,128)}, f32[128,1,8,2048]{3,0,2,1:T(8,128)}, u32[]{:S(2)}, u32[]{:S(2)}) collective-permute-start(f32[128,1,8,2048]{3,0,2,1:T(8,128)} %convolution_bitcast_fusion), channel_id=1, source_target_pairs={{0,1},{1,0},{2,3},{3,2},{4,5},{5,4},{6,7},{7,6},{8,9},{9,8},{10,11... | collective-permute-start | bytes 25165832 | tf_op jit(solution)/shard_map/ppermute | solution.py:12
  600.5 4.7 copy-start.2
  600.5 67.2 %all-to-all-start.3 = ((bf16[8,16,8,2048]{3,2,0,1:T(8,128)(2,1)}), bf16[8,16,8,2048]{3,2,0,1:T(8,128)(2,1)}, u32[]{:S(2)}, u32[]{:S(2)}) async-start(bf16[8,16,8,2048]{3,2,0,1:T(8,128)(2,1)} %copy.78), calls=%async_computation.3 | async-start | bytes 8388608 | tf_op jit(solution)/shard_map/all_to_all | solution.py:69
  667.6 4.1 copy-start.1
where the time goes:
time: 673 us; the launch traced here: 672 us
  blocking collectives  458 us (68%)
  waiting for transfers between devices  105 us (16%)
  local copies, waits for them, and re-layouts  45.7 us (7%)
  matrix products  32.2 us (5%)
  starting transfers between devices  17.1 us (3%)
  other arithmetic  13 us (2%)
    all_to_all x1, blocking collectives, on_device(): lax.all_to_all(by_rows, 'expert', split_axis=0, concat_axis=0, tiled=True)  207 us
    all_to_all x1, blocking collectives, on_device(): lax.all_to_all(result, 'expert', split_axis=0, concat_axis=0, tiled=True)  194 us
    all_to_all x1, waiting for transfers between devices, on_device(): lax.all_to_all(going_back, 'dp', split_axis=1, concat_axis=1, tiled=True)  61.6 us
    all_to_all x1, blocking collectives, on_device(): lax.all_to_all(outgoing, 'dp', split_axis=1, concat_axis=1, tiled=True)  57.9 us
    ppermute x5, waiting for transfers between devices, swapped(): return lax.ppermute(value, axis, pairs)  43.5 us
    dot_general x2, matrix products, project(): jnp.einsum('bkcf,kfd->bkcd', hidden, down_w, preferred_element_type=jnp.f...  20.9 us
  transfers between devices with their start and end apart: 6, of which 4 were waited for; matrix products, arithmetic and copies ran while one was open for 4% of the time, Pallas kernels for 0%

commit v1 on v0

--- a/solution.py
+++ b/solution.py
@@ -47,7 +47,10 @@
     dispatch = jnp.sum(matches.astype(jnp.int32), axis=2).astype(jnp.bfloat16)
     outgoing = jnp.dot(dispatch, tokens, preferred_element_type=jnp.float32).astype(jnp.bfloat16)
     outgoing = outgoing.reshape(groups, n_rows * per_slot, capacity, width)
-    by_rows = lax.all_to_all(outgoing, "dp", split_axis=1, concat_axis=1, tiled=True)
+    by_rows = jnp.concatenate(
+        lax.all_to_all(jnp.stack(jnp.split(outgoing, lax.axis_size("dp"), axis=1)), "dp", 0, 0),
+        axis=1,
+    )
     by_rows = by_rows.reshape(n_cols, subsets * per_slot, capacity, width)
     arrived = lax.all_to_all(by_rows, "expert", split_axis=0, concat_axis=0, tiled=True)
     arrived = arrived.reshape(n_cols * subsets, per_slot, capacity, width)

time: 673 us -> 666 us (0.990)
  local copies, waits for them, and re-layouts: 45.7 us -> 26.1 us
  matrix products: 32.2 us -> 39.4 us
    another operation x4, local copies, waits for them, and re-layouts: 6.95 us -> 0.05 us
where the time goes in v1:
time: 666 us; the launch traced here: 659 us
  blocking collectives  458 us (69%)
  waiting for transfers between devices  104 us (16%)
  matrix products  39.4 us (6%)
  local copies, waits for them, and re-layouts  26.1 us (4%)
  starting transfers between devices  17.6 us (3%)
  other arithmetic  13 us (2%)
    all_to_all x1, blocking collectives, on_device(): lax.all_to_all(by_rows, 'expert', split_axis=0, concat_axis=0, tiled=True)  207 us
    all_to_all x1, blocking collectives, on_device(): lax.all_to_all(result, 'expert', split_axis=0, concat_axis=0, tiled=True)  193 us
    all_to_all x1, waiting for transfers between devices, on_device(): lax.all_to_all(going_back, 'dp', split_axis=1, concat_axis=1, tiled=True)  61.2 us
    all_to_all x1, blocking collectives, on_device(): lax.all_to_all(jnp.stack(jnp.split(outgoing, lax.axis_size('dp'), axis=1)...  57.9 us
    ppermute x5, waiting for transfers between devices, swapped(): return lax.ppermute(value, axis, pairs)  43.2 us
    dot_general x2, matrix products, project(): jnp.einsum('bkcf,kfd->bkcd', hidden, down_w, preferred_element_type=jnp.f...  24.6 us
  transfers between devices with their start and end apart: 6, of which 4 were waited for; matrix products, arithmetic and copies ran while one was open for 4% of the time, Pallas kernels for 0%

profile of v1, /device:TPU:1, one launch (start us, length us, event | category | flops | bytes accessed | tf_op | source)
XLA Modules:
  0.0 659.2 jit_solution(7160546018383710596)
XLA Ops:
  6.1 57.9 %all_to_all.20 = bf16[16,8,1,8,2048]{4,3,1,2,0:T(8,128)(2,1)S(1)} all-to-all(bf16[16,8,1,8,2048]{4,3,1,2,0:T(8,128)(2,1)S(1)} %fusion.35), channel_id=1, replica_groups=mesh['dp'=16,'expert'=32] {'dp'}, dimensions={0} | all-to-all | bytes 8388608 | tf_op jit(solution)/shard_map/all_to_all | solution.py:51
  64.6 206.9 %all_to_all.21 = bf16[32,4,8,2048]{3,2,1,0:T(8,128)(2,1)S(1)} all-to-all(bf16[32,4,8,2048]{3,2,1,0:T(8,128)(2,1)S(1)} %bitcast.255), channel_id=1, replica_groups=mesh['dp'=16,'expert'=32] {'expert'}, dimensions={0} | all-to-all | bytes 8388608 | tf_op jit(solution)/shard_map/all_to_all | solution.py:55
  271.5 2.3 copy.161
  273.8 2.4 collective-permute-start.3
  276.3 1.9 collective-permute-start.1
  278.2 3.4 collective-permute-start.2
  281.6 2.4 collective-permute-start
  284.0 13.3 %collective-permute-done.1 = bf16[1,192,2048]{2,1,0:T(8,128)(2,1)S(1)} collective-permute-done((bf16[1,192,2048]{2,1,0:T(8,128)(2,1)S(1)}, bf16[1,192,2048]{2,1,0:T(8,128)(2,1)S(1)}, u32[]{:S(2)}, u32[]{:S(2)}) %collective-permute-start.1) | collective-permute-done | bytes 786464 | tf_op jit(solution)/shard_map/ppermute | solution.py:12
  297.3 3.0 fusion.3
  300.3 13.8 %collective-permute-done.2 = bf16[1,192,2048]{2,1,0:T(8,128)(2,1)S(1)} collective-permute-done((bf16[1,192,2048]{2,1,0:T(8,128)(2,1)S(1)}, bf16[1,192,2048]{2,1,0:T(8,128)(2,1)S(1)}, u32[]{:S(2)}, u32[]{:S(2)}) %collective-permute-start.2) | collective-permute-done | bytes 786464 | tf_op jit(solution)/shard_map/ppermute | solution.py:12
  315.1 16.1 %collective-permute-done = bf16[1,192,2048]{2,1,0:T(8,128)(2,1)} collective-permute-done((bf16[1,192,2048]{2,1,0:T(8,128)(2,1)S(1)}, bf16[1,192,2048]{2,1,0:T(8,128)(2,1)}, u32[]{:S(2)}, u32[]{:S(2)}) %collective-permute-start) | collective-permute-done | bytes 786464 | tf_op jit(solution)/shard_map/ppermute | solution.py:12
  331.1 10.4 %convolution_bitcast_fusion = f32[128,1,8,2048]{3,0,2,1:T(8,128)} fusion(bf16[128,1,8,2048]{3,0,2,1:T(8,128)(2,1)} %copy-done.4, f32[384,128,8]{1,0,2:T(8,128)} %fusion.3, bf16[1,192,2048]{2,1,0:T(8,128)(2,1)} %copy-done.9, bf16[1,192,2048]{2,1,0:T(8,128)(2,1)S(1)} %bitcast.264, bf16[1,192,2048]{2,1,0:T(8,128)(2,1)} %collective-permute-done, ...), kind=kOutput, calls=%fused_computation.2 | convolution fusion | flops 3229876224 | bytes 17301504 | tf_op jit(solution)/shard_map/bkcf,kfd->bkcd/dot_general | solution.py:19
  341.6 2.9 collective-permute-start.4
  344.4 9.0 %fusion.7 = f32[384,128,8]{1,0,2:T(8,128)} fusion(bf16[128,8,2048]{2,1,0:T(8,128)(2,1)} %bitcast.252, bf16[1,192,2048]{2,1,0:T(8,128)(2,1)} %copy-done.8, bf16[1,192,2048]{2,1,0:T(8,128)(2,1)S(1)} %bitcast.262), kind=kOutput, calls=%fused_computation.10 | convolution fusion | flops 1613758464 | bytes 7340032 | tf_op jit(solution)/shard_map/bkcd,kfd->bkcf/dot_general | solution.py:16
  353.4 14.2 %fusion.31 = f32[2048,128,8]{0,1,2:T(8,128)} fusion(bf16[1,192,2048]{2,1,0:T(8,128)(2,1)} %collective-permute-done, bf16[1,192,2048]{2,1,0:T(8,128)(2,1)S(1)} %bitcast.268, bf16[128,8,2048]{2,1,0:T(8,128)(2,1)} %bitcast.253, f32[384,128,8]{1,0,2:T(8,128)} %fusion.7, bf16[1,192,2048]{2,1,0:T(8,128)(2,1)} %copy-done.9, bf16[1,192,2048]{2,1,0:T(8,128)(2,1)S(1)} %bitcast.265), kind=kOutput, calls=%fused_computation.37 | convolution fusion | flops 3229876224 | bytes 17301504 | tf_op jit(solution)/shard_map/bkcf,kfd->bkcd/dot_general | solution.py:19
  367.6 9.1 %fusion = bf16[128,1,8,2048]{3,0,2,1:T(8,128)(2,1)} fusion(f32[128,1,8,2048]{3,0,2,1:T(8,128)} %collective-permute-done.4, f32[2048,128,8]{0,1,2:T(8,128)} %fusion.31), kind=kLoop, calls=%fused_computation.1 | loop fusion | flops 4194304 | bytes 20971520 | tf_op jit(solution)/shard_map/convert_element_type | solution.py:68
  376.7 7.2 %reshape.162 = bf16[32,4,8,2048]{3,1,0,2:T(4,128)(2,1)} reshape(bf16[128,1,8,2048]{3,0,2,1:T(8,128)(2,1)} %fusion) | data formatting | bytes 8388608 | tf_op jit(solution)/shard_map/reshape | solution.py:69
  383.9 4.3 copy.151
  388.2 193.3 %all_to_all.22 = bf16[32,4,8,2048]{3,1,2,0:T(4,128)(2,1)S(1)} all-to-all(bf16[32,4,8,2048]{3,1,2,0:T(4,128)(2,1)S(1)} %copy.151), channel_id=1, replica_groups=mesh['dp'=16,'expert'=32] {'expert'}, dimensions={0} | all-to-all | bytes 8388608 | tf_op jit(solution)/shard_map/all_to_all | solution.py:70
  581.5 4.4 copy.152
  585.9 2.3 copy.153
  588.2 4.7 all-to-all-start.3
  593.7 61.2 %all-to-all-done.3 = bf16[8,16,8,2048]{3,2,0,1:T(8,128)(2,1)} async-done(((bf16[8,16,8,2048]{3,2,0,1:T(8,128)(2,1)}), bf16[8,16,8,2048]{3,2,0,1:T(8,128)(2,1)}, u32[]{:S(2)}, u32[]{:S(2)}) %all-to-all-start.3) | async-done | bytes 4194336 | tf_op jit(solution)/shard_map/all_to_all | solution.py:72
  654.9 2.5 copy.154
  (59 shorter events, 9.8 us)
Async XLA Ops:
  0.0 4.4 copy-start
  271.5 2.3 copy-start.2
  271.5 4.7 copy-start.5
  271.5 6.7 %copy-start.6 = (bf16[1,1,1,192,2048]{4,3,2,1,0:T(8,128)(2,1)S(1)}, bf16[1,1,1,192,2048]{4,3,2,1,0:T(8,128)(2,1)}, u32[]{:S(2)}) copy-start(bf16[1,1,1,192,2048]{4,3,2,1,0:T(8,128)(2,1)} %param.12) | copy-start | bytes 2359300
  271.5 10.1 %copy-start.7 = (bf16[1,1,1,192,2048]{4,3,2,1,0:T(8,128)(2,1)S(1)}, bf16[1,1,1,192,2048]{4,3,2,1,0:T(8,128)(2,1)}, u32[]{:S(2)}) copy-start(bf16[1,1,1,192,2048]{4,3,2,1,0:T(8,128)(2,1)} %param.13) | copy-start | bytes 2359300
  273.8 23.5 %collective-permute-start.3 = (bf16[128,1,8,2048]{3,0,2,1:T(8,128)(2,1)S(1)}, bf16[128,1,8,2048]{3,0,2,1:T(8,128)(2,1)S(1)}, u32[]{:S(2)}, u32[]{:S(2)}) collective-permute-start(bf16[128,1,8,2048]{3,0,2,1:T(8,128)(2,1)S(1)} %copy.161), channel_id=1, source_target_pairs={{0,1},{1,0},{2,3},{3,2},{4,5},{5,4},{6,7},{7,6},{8,9},{9,8},{10,11... | collective-permute-start | bytes 12582920 | tf_op jit(solution)/shard_map/ppermute | solution.py:12
  276.3 21.1 %collective-permute-start.1 = (bf16[1,192,2048]{2,1,0:T(8,128)(2,1)S(1)}, bf16[1,192,2048]{2,1,0:T(8,128)(2,1)S(1)}, u32[]{:S(2)}, u32[]{:S(2)}) collective-permute-start(bf16[1,192,2048]{2,1,0:T(8,128)(2,1)S(1)} %bitcast.260), channel_id=1, source_target_pairs={{0,2},{1,3},{2,0},{3,1},{4,6},{5,7},{6,4},{7,5},{8,10},{9,11},{10,... | collective-permute-start | bytes 2359304 | tf_op jit(solution)/shard_map/ppermute | solution.py:12
  278.2 36.0 %collective-permute-start.2 = (bf16[1,192,2048]{2,1,0:T(8,128)(2,1)S(1)}, bf16[1,192,2048]{2,1,0:T(8,128)(2,1)S(1)}, u32[]{:S(2)}, u32[]{:S(2)}) collective-permute-start(bf16[1,192,2048]{2,1,0:T(8,128)(2,1)S(1)} %bitcast.263), channel_id=1, source_target_pairs={{0,2},{1,3},{2,0},{3,1},{4,6},{5,7},{6,4},{7,5},{8,10},{9,11},{10,... | collective-permute-start | bytes 2359304 | tf_op jit(solution)/shard_map/ppermute | solution.py:12
  281.6 49.5 %collective-permute-start = (bf16[1,192,2048]{2,1,0:T(8,128)(2,1)S(1)}, bf16[1,192,2048]{2,1,0:T(8,128)(2,1)}, u32[]{:S(2)}, u32[]{:S(2)}) collective-permute-start(bf16[1,192,2048]{2,1,0:T(8,128)(2,1)S(1)} %bitcast.266), channel_id=1, source_target_pairs={{0,2},{1,3},{2,0},{3,1},{4,6},{5,7},{6,4},{7,5},{8,10},{9,11},{10,... | collective-permute-start | bytes 2359304 | tf_op jit(solution)/shard_map/ppermute | solution.py:12
  297.3 3.0 copy-start.8
  297.3 3.0 copy-start.4
  314.2 0.9 copy-start.9
  341.6 26.0 %collective-permute-start.4 = (f32[128,1,8,2048]{3,0,2,1:T(8,128)}, f32[128,1,8,2048]{3,0,2,1:T(8,128)}, u32[]{:S(2)}, u32[]{:S(2)}) collective-permute-start(f32[128,1,8,2048]{3,0,2,1:T(8,128)} %convolution_bitcast_fusion), channel_id=1, source_target_pairs={{0,1},{1,0},{2,3},{3,2},{4,5},{5,4},{6,7},{7,6},{8,9},{9,8},{10,11... | collective-permute-start | bytes 25165832 | tf_op jit(solution)/shard_map/ppermute | solution.py:12
  588.2 4.7 copy-start.3
  588.2 66.7 %all-to-all-start.3 = ((bf16[8,16,8,2048]{3,2,0,1:T(8,128)(2,1)}), bf16[8,16,8,2048]{3,2,0,1:T(8,128)(2,1)}, u32[]{:S(2)}, u32[]{:S(2)}) async-start(bf16[8,16,8,2048]{3,2,0,1:T(8,128)(2,1)} %copy.153), calls=%async_computation.3 | async-start | bytes 8388608 | tf_op jit(solution)/shard_map/all_to_all | solution.py:72
  654.9 4.1 copy-start.1
